TPU v7x, 32 devices: a whole 2x2x4 slice. The times are simulated.
32 devices in a mesh: wide: 16 (over z, y, x), narrow: 2 (over core).
Axes of the slice: x: 2, y: 2, z: 4, core: 2. Of those that a mesh axis runs over, the one named last changes fastest.
Arguments:
- rhs: float32 [384, 64, 128], P(('wide', 'narrow')), may hold values from -8 to 8
- pivot_inv: float32 [384, 128, 128], P(('wide', 'narrow')), may hold values from -0.5 to 0.5
- lower_gain: float32 [384, 128, 128], P(('wide', 'narrow')), may hold values from -1 to 1
- upper_gain: float32 [384, 128, 128], P(('wide', 'narrow')), may hold values from -1 to 1
Outputs:
- solution: float32 [384, 64, 128], P(('wide', 'narrow'))
All inputs are finite; a program needn't handle non-finite values.
Results may differ from a plain program's by a relative error of at most 0.0003.
Values sent between devices are 32-bit elements; how exact they have to be, the bound alone decides.
A program may use at most 128 MiB of HBM per device.

v0:
```python
import jax
import jax.numpy as jnp
from jax import lax
from jax.sharding import PartitionSpec as P


def prefix(value, axis, join, neutral, backward):
    count, mine = (lax.axis_size(axis), lax.axis_index(axis))
    pieces = jax.tree.map(lambda part: lax.all_gather(part, axis), value)
    if backward:
        pieces = jax.tree.map(lambda part: part[::-1], pieces)
        mine = count - 1 - mine
    subtotal = jax.tree.map(
        lambda part, zero: jnp.full_like(part, 0) + jnp.asarray(zero, part.dtype), value, neutral
    )

    def step(position, subtotal):
        longer = join(subtotal, jax.tree.map(lambda part: part[position], pieces))
        return jax.tree.map(lambda new, old: jnp.where(position < mine, new, old), longer, subtotal)

    return lax.fori_loop(0, count - 1, step, subtotal)


def compose(earlier, later):
    highest = lax.Precision.HIGHEST
    early_map, early_off = earlier
    late_map, late_off = later
    joined_map = jnp.einsum("...ij,...jk->...ik", early_map, late_map, precision=highest)
    joined_off = jnp.einsum("...ij,...jk->...ik", early_off, late_map, precision=highest) + late_off
    return (joined_map, joined_off)


def chain_prefix(own, reverse):
    identity = (jnp.eye(own[0].shape[0], dtype=jnp.float32), jnp.zeros(own[1].shape, jnp.float32))
    return prefix(own, ("wide", "narrow"), compose, identity, reverse)


def on_device(rhs, pivot_inv, lower_gain, upper_gain):
    highest = lax.Precision.HIGHEST
    scaled = jnp.einsum("krb,kbc->krc", rhs, pivot_inv, precision=highest)
    down_map, down_off = lax.associative_scan(compose, (-lower_gain, scaled))
    before = chain_prefix((down_map[-1], down_off[-1]), False)
    forward = down_off + jnp.einsum("rb,kbc->krc", before[1], down_map, precision=highest)
    back_map, back_off = lax.associative_scan(
        compose, (-jnp.flip(upper_gain, 0), jnp.flip(forward, 0))
    )
    after = chain_prefix((back_map[-1], back_off[-1]), True)
    reversed_solution = back_off + jnp.einsum("rb,kbc->krc", after[1], back_map, precision=highest)
    return jnp.flip(reversed_solution, 0)


def solution(mesh):
    placed = (
        P(("wide", "narrow"), None, None),
        P(("wide", "narrow"), None, None),
        P(("wide", "narrow"), None, None),
        P(("wide", "narrow"), None, None),
    )
    return jax.shard_map(
        on_device,
        mesh=mesh,
        in_specs=placed,
        out_specs=P(("wide", "narrow"), None, None),
        check_vma=False,
    )
```

profile of v0, /device:TPU:0, one launch (start us, length us, event | category | flops | bytes accessed | tf_op | source)
XLA Modules:
  0.0 329.2 jit_solution(1720111624600092272)
XLA Ops:
  25.0 2.6 pad.98
  28.3 40.7 %all-gather.7.cloned.1.call-done = f32[32,64,128]{2,1,0:T(8,128)} async-done(((f32[1,64,128]{2,1,0:T(8,128)}), f32[32,64,128]{2,1,0:T(8,128)}) %all-gather.7.cloned.1.call-update) | async-done | bytes 1048592 | tf_op jit(solution)/shard_map/all_gather | solution.py:9
  69.1 58.2 %all-gather.5.cloned.1.call-done = f32[32,128,128]{2,1,0:T(8,128)} async-done(((f32[1,128,128]{2,1,0:T(8,128)}), f32[32,128,128]{2,1,0:T(8,128)}) %all-gather.5.cloned.1.call-update) | async-done | bytes 2097168 | tf_op jit(solution)/shard_map/all_gather | solution.py:9
  127.3 74.5 %while.28 = (s32[]{:T(128)}, f32[64,128]{1,0:T(8,128)}, s32[]{:T(128)}, f32[32,128,128]{2,1,0:T(8,128)}, f32[32,64,128]{2,1,0:T(8,128)}, /*index=5*/s32[]{:T(128)}, s32[]{:T(128)}) while((s32[]{:T(128)}, f32[64,128]{1,0:T(8,128)}, s32[]{:T(128)}, f32[32,128,128]{2,1,0:T(8,128)}, f32[32,64,128]{2,1,0:T(8,128)}, ...), condition=%wide.region_1.2_spmd.clone, body=%wide.region_0.1_spmd.clone.sunk | while | flops 12615684 | bytes 264799 | solution.py:21
  132.8 1.6 fusion.94
  135.2 1.6 fusion.94
  137.6 1.6 fusion.94
  140.0 1.6 fusion.94
  142.4 1.6 fusion.94
  147.3 1.6 fusion.94
  159.3 1.6 fusion.94
  161.7 1.6 fusion.94
  176.1 1.6 fusion.94
  180.9 1.6 fusion.94
  183.3 1.6 fusion.94
  195.3 1.6 fusion.94
  201.7 2.2 fusion.18
  214.5 2.0 pad.88
  218.1 2.9 pad.91
  225.4 2.6 pad.93
  231.6 3.1 rev.16
  234.7 49.5 %all-gather.11.cloned.1.call-done = f32[32,64,128]{2,1,0:T(8,128)} async-done(((f32[1,64,128]{2,1,0:T(8,128)}), f32[32,64,128]{2,1,0:T(8,128)}) %all-gather.11.cloned.1.call-update) | async-done | bytes 1048592 | tf_op jit(solution)/shard_map/all_gather | solution.py:9
  284.3 2.4 rev.17
  286.6 33.3 %while.29 = (s32[]{:T(128)}, f32[64,128]{1,0:T(8,128)S(1)}, s32[]{:T(128)}, f32[32,128,128]{2,1,0:T(8,128)}, f32[32,64,128]{2,1,0:T(8,128)}, /*index=5*/s32[]{:T(128)}, s32[]{:T(128)}) while((s32[]{:T(128)}, f32[64,128]{1,0:T(8,128)S(1)}, s32[]{:T(128)}, f32[32,128,128]{2,1,0:T(8,128)}, f32[32,64,128]{2,1,0:T(8,128)}, ...), condition=%wide.region_3.4_spmd.clone, body=%wide.region_2.3_spmd.clone.sunk | while | flops 12615684 | bytes 264799 | solution.py:21
  (233 shorter events, 128.2 us)
Async XLA Ops:
  6.5 1.8 copy-start
  6.5 1.8 copy-start.9
  6.5 62.5 %all-gather.7.cloned.1.call-start = ((), (), s32[]{:S(2)}) async-start(), calls=%async_computation.1 | async-start | bytes 1081344 | tf_op jit(solution)/shard_map/all_gather | solution.py:9
  11.7 3.9 %copy-start.4 = (f32[12,64,128]{2,1,0:T(8,128)}, f32[12,64,128]{2,1,0:T(8,128)S(1)}, u32[]{:S(2)}) copy-start(f32[12,64,128]{2,1,0:T(8,128)S(1)} %pad.81) | copy-start | bytes 1179652
  11.8 3.9 %copy-start.5 = (f32[12,64,128]{2,1,0:T(8,128)}, f32[12,64,128]{2,1,0:T(8,128)S(1)}, u32[]{:S(2)}) copy-start(f32[12,64,128]{2,1,0:T(8,128)S(1)} %pad.80) | copy-start | bytes 1179652
  12.5 114.7 %all-gather.5.cloned.1.call-start = ((), (), s32[]{:S(2)}) async-start(), calls=%async_computation | async-start | bytes 2162688 | tf_op jit(solution)/shard_map/all_gather | solution.py:9
  15.8 2.2 copy-start.1
  17.2 4.4 %copy-start.2 = (f32[12,128,128]{2,1,0:T(8,128)}, f32[12,128,128]{2,1,0:T(8,128)S(1)}, u32[]{:S(2)}) copy-start(f32[12,128,128]{2,1,0:T(8,128)S(1)} %pad.86) | copy-start | bytes 2359300
  18.0 213.6 %all-gather.9.cloned.1.call-start = ((), (), s32[]{:S(2)}) async-start(), calls=%async_computation.2 | async-start | bytes 2162688 | tf_op jit(solution)/shard_map/all_gather | solution.py:9
  21.4 1.3 copy-start.3
  21.8 0.8 copy-start.11
  28.3 256.0 %all-gather.11.cloned.1.call-start = ((), (), s32[]{:S(2)}) async-start(), calls=%async_computation.3 | async-start | bytes 1081344 | tf_op jit(solution)/shard_map/all_gather | solution.py:9
  210.7 0.7 copy-start.8
  212.8 1.1 copy-start.10
  234.7 85.8 %copy-start.6 = (f32[12,64,128]{2,1,0:T(8,128)S(1)}, f32[12,64,128]{2,1,0:T(8,128)}, u32[]{:S(2)}) copy-start(f32[12,64,128]{2,1,0:T(8,128)} %pad.93) | copy-start | bytes 1179652
  319.9 0.6 copy-start.7
Sparse Core Ops, SparseCore 0:
  12.7 56.3 all-gather.6
  71.9 55.3 all-gather.4
  130.1 55.3 all-gather.8
  231.7 52.5 all-gather.10
where the time goes:
time: 336 us; the launch traced here: 329 us
  waiting for transfers between devices  149 us (44%)
  matrix products  99.3 us (30%)
  local copies, waits for them, and re-layouts  52.1 us (16%)
  other arithmetic  14.1 us (4%)
  between operations  13.8 us (4%)
    all_gather x4, waiting for transfers between devices, prefix(): pieces = jax.tree.map(lambda part: lax.all_gather(part, axis), value)  149 us
    dot_general x74, matrix products, compose(): jnp.einsum('...ij,...jk->...ik', early_off, late_map, precision=highest)  91 us
    while x62, local copies, waits for them, and re-layouts  23.6 us
    pad x10, local copies, waits for them, and re-layouts, on_device(): lax.associative_scan(compose, (-jnp.flip(upper_gain, 0), jnp.flip(forward...  10.5 us
    slice x11, local copies, waits for them, and re-layouts, on_device(): lax.associative_scan(compose, (-jnp.flip(upper_gain, 0), jnp.flip(forward...  8.84 us
  transfers between devices with their start and end apart: 4, of which 3 were waited for; matrix products, arithmetic and copies ran while one was open for 37% of the time, Pallas kernels for 0%

commit v1 on v0

v1 whole, which is shorter than its diff:
```python
import functools

import jax
import jax.numpy as jnp
from jax import lax
from jax.experimental import pallas as pl
from jax.experimental.pallas import tpu as pltpu
from jax.sharding import PartitionSpec as P

MESH = pl.DeviceIdType.MESH


def halves(value):
    high = value.astype(jnp.bfloat16)
    low = (value - high.astype(jnp.float32)).astype(jnp.bfloat16)
    return high, low


def right_side(value):
    high, low = halves(value)
    row = jnp.concatenate([high, low], axis=1)
    return jnp.concatenate([row, row], axis=0)


def left_side(value):
    high, low = halves(value)
    return jnp.concatenate([high, low], axis=1)


def fold(value, width):
    return value[:, :width] + value[:, width:]


def product(left, right):
    wide = jnp.dot(left_side(left), right_side(right), preferred_element_type=jnp.float32)
    return fold(wide, right.shape[1])


def kernel(
    levels, rhs, pivot, lower, upper, out, ahead, tails, maps, group, fp, fq, fs, send_sem, recv_sem
):
    rows, sides, size = rhs.shape
    m0, c0, w0, b0, n0, end = 0, size, size + sides, 2 * size + sides, 2 * (size + sides), 3 * size + 2 * sides
    names = ("wide", "narrow")
    place = {name: lax.axis_index(name) for name in names}

    def partner(level):
        axis, stride = levels[level]
        mine = place[axis]
        side = lax.rem(lax.div(mine, stride), 2)
        other = mine + stride - 2 * stride * side
        return side, tuple(other if name == axis else place[name] for name in names)

    barrier = pltpu.get_barrier_semaphore()
    for level in range(len(levels)):
        pl.semaphore_signal(barrier, inc=1, device_id=partner(level)[1], device_id_type=MESH)

    scaled = [product(rhs[i], pivot[i]) for i in range(rows)]
    front = jnp.concatenate([-lower[0], scaled[0]], axis=0)
    ahead[0] = front
    back = -upper[rows - 1]
    tails[rows - 1, size + sides :] = back
    for i in range(1, rows):
        step = product(front, lower[i])
        front = jnp.concatenate([-step[:size], scaled[i] - step[size:]], axis=0)
        ahead[i] = front
        back = -product(back, upper[rows - 1 - i])
        tails[rows - 1 - i, size + sides :] = back
    total = front
    tails[rows - 1, : size + sides] = total
    for i in range(rows - 2, -1, -1):
        total = ahead[i] - product(total, upper[i])
        tails[i, : size + sides] = total

    pl.semaphore_wait(barrier, len(levels))

    def exchange(level):
        side, other = partner(level)
        span = pl.ds(c0, n0 - c0) if level == len(levels) - 1 else pl.ds(0, end)
        return pltpu.make_async_remote_copy(
            src_ref=group.at[level, side, span],
            dst_ref=group.at[level, side, span],
            send_sem=send_sem.at[level],
            recv_sem=recv_sem.at[level],
            device_id=other,
            device_id_type=MESH,
        )

    side = partner(0)[0]
    group[0, side, :c0] = ahead[rows - 1, :size]
    group[0, side, c0:w0] = ahead[rows - 1, size:]
    group[0, side, w0:n0] = tails[0, : size + sides]
    group[0, side, n0:] = tails[0, size + sides :]
    copy = exchange(0)
    copy.start()

    for i in range(rows):
        w_high, w_low = halves(tails[i, :size])
        n_high, n_low = halves(tails[i, size + sides :])
        maps[i] = jnp.concatenate(
            [jnp.concatenate([w_high, w_low], axis=1), jnp.concatenate([n_high, n_low], axis=1)], axis=0
        )
    eye = (
        lax.broadcasted_iota(jnp.int32, (size, size), 0) == lax.broadcasted_iota(jnp.int32, (size, size), 1)
    ).astype(jnp.float32)
    fp[:size] = eye
    fp[size:] = jnp.zeros((sides, size), jnp.float32)
    fq[...] = eye
    fs[...] = jnp.zeros((size + sides, size), jnp.float32)

    for level in range(len(levels) - 1):
        copy.wait()
        side = partner(level)[0]
        first, second = group.at[level, 0], group.at[level, 1]
        front = first[m0:w0]
        joined = jnp.dot(
            left_side(front),
            jnp.concatenate([right_side(second[m0:c0]), right_side(second[w0:b0])], axis=1),
            preferred_element_type=jnp.float32,
        )
        onward = fold(joined[:, : 2 * size], size)
        turned = fold(joined[:, 2 * size :], size)
        turned = jnp.concatenate([turned[:size], turned[size:] + second[b0:n0]], axis=0)
        returned = product(jnp.concatenate([turned, second[n0:]], axis=0), first[n0:])
        following = partner(level + 1)[0]
        group[level + 1, following, m0:c0] = onward[:size]
        group[level + 1, following, c0:w0] = onward[size:] + second[c0:w0]
        group[level + 1, following, w0:n0] = first[w0:n0] + returned[: size + sides]
        group[level + 1, following, n0:] = returned[size + sides :]
        copy = exchange(level + 1)
        copy.start()

        @pl.when(side == 0)
        def _():
            more = product(jnp.concatenate([turned, second[n0:]], axis=0), fq[...])
            fs[...] = fs[...] + more[: size + sides]
            fq[...] = more[size + sides :]

        @pl.when(side == 1)
        def _():
            more = product(front, fp[:size])
            fp[size:] = fp[size:] + more[size:]
            fp[:size] = more[:size]
            more = product(front, fs[:size])
            fs[size:] = fs[size:] + more[size:]
            fs[:size] = more[:size]

    copy.wait()
    level = len(levels) - 1
    side = partner(level)[0]
    enter = group[level, 0, c0:w0]
    leave = product(enter, group[level, 1, w0:b0]) + group[level, 1, b0:n0]
    enter = jnp.where(side == 1, enter, 0.0)
    leave = jnp.where(side == 0, leave, 0.0)
    x_in = product(enter, fp[:size]) + fp[size:]
    y_in = product(leave, fq[...]) + product(enter, fs[:size]) + fs[size:]
    x_high, x_low = halves(x_in)
    y_high, y_low = halves(y_in)
    left = jnp.concatenate(
        [jnp.concatenate([x_high, y_high], axis=1), jnp.concatenate([x_low, y_low], axis=1)], axis=0
    )
    for i in range(rows):
        both = fold(jnp.dot(left, maps[i], preferred_element_type=jnp.float32), size)
        out[i] = tails[i, size : size + sides] + both[:sides] + both[sides:]


def on_device(levels, rhs, pivot_inv, lower_gain, upper_gain):
    rows, sides, size = rhs.shape
    depth = len(levels)
    span = 3 * size + 2 * sides
    whole = pl.BlockSpec(memory_space=pltpu.VMEM)
    return pl.pallas_call(
        functools.partial(kernel, levels),
        out_shape=jax.ShapeDtypeStruct(rhs.shape, jnp.float32),
        in_specs=[whole] * 4,
        out_specs=whole,
        scratch_shapes=[
            pltpu.VMEM((rows, size + sides, size), jnp.float32),
            pltpu.VMEM((rows, 2 * size + sides, size), jnp.float32),
            pltpu.VMEM((rows, 2 * size, 2 * size), jnp.bfloat16),
            pltpu.VMEM((depth, 2, span, size), jnp.float32),
            pltpu.VMEM((size + sides, size), jnp.float32),
            pltpu.VMEM((size, size), jnp.float32),
            pltpu.VMEM((size + sides, size), jnp.float32),
            pltpu.SemaphoreType.DMA((depth,)),
            pltpu.SemaphoreType.DMA((depth,)),
        ],
        compiler_params=pltpu.CompilerParams(
            collective_id=0, has_side_effects=True, vmem_limit_bytes=40 * 2**20
        ),
    )(rhs, pivot_inv, lower_gain, upper_gain)


def solution(mesh):
    levels = []
    for axis in ("narrow", "wide"):
        stride = 1
        while stride < mesh.shape[axis]:
            levels.append((axis, stride))
            stride *= 2
    placed = P(("wide", "narrow"), None, None)
    return jax.shard_map(
        functools.partial(on_device, tuple(levels)),
        mesh=mesh,
        in_specs=(placed,) * 4,
        out_specs=placed,
        check_vma=False,
    )
```

time: 336 us -> 44.3 us (0.13); the launches traced: 329 us -> 44 us
  waiting for transfers between devices: 149 us -> 0 us
  matrix products: 99.3 us -> 0 us
  local copies, waits for them, and re-layouts: 52.1 us -> 5.14 us
  Pallas kernels: 0 us -> 38.8 us
  other arithmetic: 14.1 us -> 0 us
  between operations: 13.8 us -> 0.01 us
    all_gather x4 -> x0, waiting for transfers between devices: 149 us -> none  [prefix(): pieces = jax.tree.map(lambda part: lax.all_gather(part, axis), value)]
    dot_general x89 -> x0, matrix products: 99.3 us -> none  [the longest x74 91 us: compose(): jnp.einsum('...ij,...jk->...ik', early_off, late_map, precision=highest)]
    pallas_call x0 -> x1, Pallas kernels: none -> 38.8 us  [on_device(): pl.pallas_call(functools.partial(kernel, levels), out_shape=jax.ShapeDtyp...]
    while x62 -> x0, local copies, waits for them, and re-layouts: 23.6 us -> none
    pad x20 -> x0, local copies, waits for them, and re-layouts: 11 us -> none  [the longest x10 10.5 us: on_device(): lax.associative_scan(compose, (-jnp.flip(upper_gain, 0), jnp.flip(forward...]
    slice x17 -> x0, local copies, waits for them, and re-layouts: 10.1 us -> none  [the longest x11 8.84 us: on_device(): lax.associative_scan(compose, (-jnp.flip(upper_gain, 0), jnp.flip(forward...]
    rev x3 -> x0, local copies, waits for them, and re-layouts: 6.24 us -> none  [the longest x2 5.47 us: prefix(): pieces = jax.tree.map(lambda part: part[::-1], pieces)]
    add x12 -> x0, other arithmetic: 6.08 us -> none  [the longest x6 4.58 us: on_device(): lax.associative_scan(compose, (-jnp.flip(upper_gain, 0), jnp.flip(forward...]
  transfers between devices with their start and end apart: 4 -> 0, of which waited for: 3 -> 0; matrix products, arithmetic and copies ran while one was open for 37% -> 0% of each run, Pallas kernels for 0% -> 0%
where the time goes in v1:
time: 44.3 us; the launch traced here: 44 us
  Pallas kernels  38.8 us (88%)
  local copies, waits for them, and re-layouts  5.14 us (12%)
    pallas_call x1, Pallas kernels, on_device(): pl.pallas_call(functools.partial(kernel, levels), out_shape=jax.ShapeDtyp...  38.8 us
    unnamed x9, local copies, waits for them, and re-layouts  5.14 us

profile of v1, /device:TPU:0, one launch (start us, length us, event | category | flops | bytes accessed | tf_op | source)
XLA Modules:
  0.0 44.0 jit_solution(4940499234161817888)
XLA Ops:
  0.0 0.0 copy-start
  0.0 1.1 %copy-done = f32[12,128,128]{2,1,0:T(8,128)S(1)} copy-done((f32[12,128,128]{2,1,0:T(8,128)S(1)}, f32[12,128,128]{2,1,0:T(8,128)}, u32[]{:S(2)}) %copy-start) | copy-done | bytes 786456
  1.1 0.0 copy-start.1
  1.1 1.1 %copy-done.1 = f32[12,128,128]{2,1,0:T(8,128)S(1)} copy-done((f32[12,128,128]{2,1,0:T(8,128)S(1)}, f32[12,128,128]{2,1,0:T(8,128)}, u32[]{:S(2)}) %copy-start.1) | copy-done | bytes 786456
  2.3 0.0 copy-start.2
  2.3 1.1 %copy-done.2 = f32[12,128,128]{2,1,0:T(8,128)S(1)} copy-done((f32[12,128,128]{2,1,0:T(8,128)S(1)}, f32[12,128,128]{2,1,0:T(8,128)}, u32[]{:S(2)}) %copy-start.2) | copy-done | bytes 786456
  3.4 0.0 copy-start.3
  3.4 1.0 %copy-done.3 = f32[12,64,128]{2,1,0:T(8,128)S(1)} copy-done((f32[12,64,128]{2,1,0:T(8,128)S(1)}, f32[12,64,128]{2,1,0:T(8,128)}, u32[]{:S(2)}) %copy-start.3) | copy-done | bytes 393240
  4.4 38.8 %shard_map.46 = f32[12,64,128]{2,1,0:T(8,128)S(1)} custom-call(f32[12,64,128]{2,1,0:T(8,128)S(1)} %copy-done.3, f32[12,128,128]{2,1,0:T(8,128)S(1)} %copy-done, f32[12,128,128]{2,1,0:T(8,128)S(1)} %copy-done.1, f32[12,128,128]{2,1,0:T(8,128)S(1)} %copy-done.2), custom_call_target="tpu_custom_call" | custom-call | tf_op jit(solution)/shard_map/pallas_call | solution.py:172
  43.3 0.7 %copy.6 = f32[12,64,128]{2,1,0:T(8,128)} copy(f32[12,64,128]{2,1,0:T(8,128)S(1)} %shard_map.46) | data formatting | bytes 786432
Async XLA Ops:
  0.0 1.1 %copy-start = (f32[12,128,128]{2,1,0:T(8,128)S(1)}, f32[12,128,128]{2,1,0:T(8,128)}, u32[]{:S(2)}) copy-start(f32[12,128,128]{2,1,0:T(8,128)} %pivot.1) | copy-start | bytes 2359300
  1.1 1.1 %copy-start.1 = (f32[12,128,128]{2,1,0:T(8,128)S(1)}, f32[12,128,128]{2,1,0:T(8,128)}, u32[]{:S(2)}) copy-start(f32[12,128,128]{2,1,0:T(8,128)} %lower.1) | copy-start | bytes 2359300
  2.3 1.1 %copy-start.2 = (f32[12,128,128]{2,1,0:T(8,128)S(1)}, f32[12,128,128]{2,1,0:T(8,128)}, u32[]{:S(2)}) copy-start(f32[12,128,128]{2,1,0:T(8,128)} %upper.1) | copy-start | bytes 2359300
  3.4 1.0 %copy-start.3 = (f32[12,64,128]{2,1,0:T(8,128)S(1)}, f32[12,64,128]{2,1,0:T(8,128)}, u32[]{:S(2)}) copy-start(f32[12,64,128]{2,1,0:T(8,128)} %rhs.1) | copy-start | bytes 1179652

commit v2 on v1

v2 whole, which is shorter than its diff:
```python
import functools

import jax
import jax.numpy as jnp
from jax import lax
from jax.experimental import pallas as pl
from jax.experimental.pallas import tpu as pltpu
from jax.sharding import PartitionSpec as P

MESH = pl.DeviceIdType.MESH
PIECE = 3
PARTS = 2


def halves(value):
    high = value.astype(jnp.bfloat16)
    low = (value - high.astype(jnp.float32)).astype(jnp.bfloat16)
    return high, low


def right_side(value):
    high, low = halves(value)
    row = jnp.concatenate([high, low], axis=1)
    return jnp.concatenate([row, row], axis=0)


def left_side(value):
    high, low = halves(value)
    return jnp.concatenate([high, low], axis=1)


def fold(value, width):
    return value[:, :width] + value[:, width:]


def product(left, right):
    wide = jnp.dot(left_side(left), right_side(right), preferred_element_type=jnp.float32)
    return fold(wide, right.shape[1])


def kernel(
    levels,
    planes,
    rhs_hbm,
    pivot_hbm,
    lower_hbm,
    upper_hbm,
    out,
    rhs,
    pivot,
    lower,
    upper,
    ahead,
    tails,
    maps,
    group,
    fp,
    fq,
    fs,
    enter,
    leave,
    met,
    enter_on,
    leave_on,
    met_on,
    load_sem,
    send_sem,
    recv_sem,
    pass_send_sem,
    pass_recv_sem,
    chain_send_sem,
    chain_recv_sem,
):
    rows, sides, size = rhs.shape
    m0, c0, w0, b0, n0, end = 0, size, size + sides, 2 * size + sides, 2 * (size + sides), 3 * size + 2 * sides
    names = ("wide", "narrow")
    place = {name: lax.axis_index(name) for name in names}
    depth = len(levels)

    loads = {}
    pieces = rows // PIECE
    for step in range(pieces):
        for kind, (source, target) in enumerate(
            ((rhs_hbm, rhs), (pivot_hbm, pivot), (lower_hbm, lower), (upper_hbm, upper))
        ):
            piece = pieces - 1 - step if kind == 3 else step
            span = pl.ds(piece * PIECE, PIECE)
            load = pltpu.make_async_copy(source.at[span], target.at[span], load_sem.at[kind, piece])
            load.start()
            loads[kind, step] = load

    def partner(level):
        axis, stride = levels[level]
        mine = place[axis]
        side = lax.rem(lax.div(mine, stride), 2)
        other = mine + stride - 2 * stride * side
        return side, tuple(other if name == axis else place[name] for name in names)

    hop = lax.axis_size("wide") // planes
    plane = lax.div(place["wide"], hop)
    before = (place["wide"] - hop, place["narrow"])
    after = (place["wide"] + hop, place["narrow"])
    sibling = (place["wide"], 1 - place["narrow"])

    barrier = pltpu.get_barrier_semaphore()
    for level in range(depth):
        pl.semaphore_signal(barrier, inc=1, device_id=partner(level)[1], device_id_type=MESH)

    @pl.when(plane > 0)
    def _():
        pl.semaphore_signal(barrier, inc=1, device_id=before, device_id_type=MESH)

    @pl.when(plane < planes - 1)
    def _():
        pl.semaphore_signal(barrier, inc=1, device_id=after, device_id_type=MESH)

    for i in range(rows):
        if i % PIECE == 0:
            for kind in range(4):
                loads[kind, i // PIECE].wait()
        scaled = product(rhs[i], pivot[i])
        if i == 0:
            front = jnp.concatenate([-lower[0], scaled], axis=0)
            back = -upper[rows - 1]
        else:
            step = product(front, lower[i])
            front = jnp.concatenate([-step[:size], scaled - step[size:]], axis=0)
            back = -product(back, upper[rows - 1 - i])
        ahead[i] = front
        tails[rows - 1 - i, size + sides :] = back
    total = front
    tails[rows - 1, : size + sides] = total
    for i in range(rows - 2, -1, -1):
        total = ahead[i] - product(total, upper[i])
        tails[i, : size + sides] = total

    inner = (plane > 0).astype(jnp.int32) + (plane < planes - 1).astype(jnp.int32)
    pl.semaphore_wait(barrier, depth + inner)

    part = end // (2 * PARTS)

    def exchange(level):
        side, other = partner(level)
        if levels[level][0] == "narrow":
            spans = [pl.ds(0, end)]
        else:
            begin = place["narrow"] * (end // 2)
            spans = [pl.ds(pl.multiple_of(begin + k * part, part), part) for k in range(PARTS)]
        return [
            pltpu.make_async_remote_copy(
                src_ref=group.at[level, side, span],
                dst_ref=group.at[level, side, span],
                send_sem=send_sem.at[level, k],
                recv_sem=recv_sem.at[level, k],
                device_id=other,
                device_id_type=MESH,
            )
            for k, span in enumerate(spans)
        ]

    def finish(level, copies):
        if levels[level][0] == "narrow":
            copies[0].wait()
            return
        side = partner(level)[0]
        begin = place["narrow"] * (end // 2)
        relays = []
        for k, copy in enumerate(copies):
            copy.wait_recv()
            span = pl.ds(pl.multiple_of(begin + k * part, part), part)
            relay = pltpu.make_async_remote_copy(
                src_ref=group.at[level, 1 - side, span],
                dst_ref=group.at[level, 1 - side, span],
                send_sem=pass_send_sem.at[level, k],
                recv_sem=pass_recv_sem.at[level, k],
                device_id=sibling,
                device_id_type=MESH,
            )
            relay.start()
            relays.append(relay)
        for copy in copies:
            copy.wait_send()
        for relay in relays:
            relay.wait()

    side = partner(0)[0]
    group[0, side, :c0] = ahead[rows - 1, :size]
    group[0, side, c0:w0] = ahead[rows - 1, size:]
    group[0, side, w0:n0] = tails[0, : size + sides]
    group[0, side, n0:] = tails[0, size + sides :]
    copies = exchange(0)
    for copy in copies:
        copy.start()

    eye = (
        lax.broadcasted_iota(jnp.int32, (size, size), 0) == lax.broadcasted_iota(jnp.int32, (size, size), 1)
    ).astype(jnp.float32)
    fp[:size] = eye
    fp[size:] = jnp.zeros((sides, size), jnp.float32)
    fq[...] = eye
    fs[...] = jnp.zeros((size + sides, size), jnp.float32)

    def hand(kind, source, target, device):
        return pltpu.make_async_remote_copy(
            src_ref=source,
            dst_ref=target,
            send_sem=chain_send_sem.at[kind],
            recv_sem=chain_recv_sem.at[kind],
            device_id=device,
            device_id_type=MESH,
        )

    enter_right = hand(0, enter_on, enter, after)
    met_left = hand(1, met_on, met, before)
    leave_left = hand(2, leave_on, leave, before)

    for level in range(depth):
        finish(level, copies)
        side = partner(level)[0]
        first, second = group.at[level, 0], group.at[level, 1]
        front = first[m0:w0]
        joined = jnp.dot(
            left_side(front),
            jnp.concatenate([right_side(second[m0:c0]), right_side(second[w0:b0])], axis=1),
            preferred_element_type=jnp.float32,
        )
        onward = fold(joined[:, : 2 * size], size)
        turned = fold(joined[:, 2 * size :], size)
        turned = jnp.concatenate([turned[:size], turned[size:] + second[b0:n0]], axis=0)
        returned = product(jnp.concatenate([turned, second[n0:]], axis=0), first[n0:])
        following = partner(level + 1)[0] if level < depth - 1 else 0
        group[level + 1, following, m0:c0] = onward[:size]
        group[level + 1, following, c0:w0] = onward[size:] + second[c0:w0]
        group[level + 1, following, w0:n0] = first[w0:n0] + returned[: size + sides]
        group[level + 1, following, n0:] = returned[size + sides :]
        if level < depth - 1:
            copies = exchange(level + 1)
            for copy in copies:
                copy.start()
        else:

            @pl.when(plane == 0)
            def _():
                enter_on[...] = group[depth, 0, c0:w0]
                enter_right.start()

            @pl.when(plane == planes - 1)
            def _():
                met_on[...] = group[depth, 0, w0:n0]
                met_left.start()

        if level == 0:
            for i in range(rows):
                w_high, w_low = halves(tails[i, :size])
                n_high, n_low = halves(tails[i, size + sides :])
                maps[i] = jnp.concatenate(
                    [jnp.concatenate([w_high, w_low], axis=1), jnp.concatenate([n_high, n_low], axis=1)],
                    axis=0,
                )

        @pl.when(side == 0)
        def _():
            more = product(jnp.concatenate([turned, second[n0:]], axis=0), fq[...])
            fs[...] = fs[...] + more[: size + sides]
            fq[...] = more[size + sides :]

        @pl.when(side == 1)
        def _():
            more = product(front, fp[:size])
            fp[size:] = fp[size:] + more[size:]
            fp[:size] = more[:size]
            more = product(front, fs[:size])
            fs[size:] = fs[size:] + more[size:]
            fs[:size] = more[:size]

    mine = group.at[depth, 0]

    def step_left(index):
        if index == 0:
            enter[...] = jnp.zeros((sides, size), jnp.float32)
            reach = mine[c0:w0]
        else:
            enter_right.wait_recv()
            reach = product(enter[...], mine[m0:c0]) + mine[c0:w0]
            enter_on[...] = reach
            enter_right.start()
        if index == planes // 2 - 1:
            if index > 0:
                partial = product(enter[...], mine[w0:b0]) + mine[b0:n0]
            met_left.wait_recv()
            leave[...] = product(reach, met[:size]) + met[size:]
        else:
            if index > 0:
                partial = product(enter[...], mine[w0:b0]) + mine[b0:n0]
            leave_left.wait_recv()
        if index > 0:
            leave_on[...] = product(leave[...], mine[n0:]) + partial
            leave_left.start()
            leave_left.wait_send()
        enter_right.wait_send()

    def step_right(index):
        if index < planes - 1:
            met_left.wait_recv()
            turned = product(mine[m0:w0], met[:size])
            turned = jnp.concatenate([turned[:size], turned[size:] + met[size:]], axis=0)
            met_on[...] = product(turned, mine[n0:]) + mine[w0:n0]
            met_left.start()
        enter_right.wait_recv()
        if index < planes - 1:
            reach = product(enter[...], mine[m0:c0]) + mine[c0:w0]
            enter_on[...] = reach
            enter_right.start()
            leave[...] = product(reach, met[:size]) + met[size:]
            enter_right.wait_send()
        else:
            leave[...] = jnp.zeros((sides, size), jnp.float32)
        met_left.wait_send()

    for index in range(planes):
        pl.when(plane == index)(functools.partial(step_left if index < planes // 2 else step_right, index))

    x_in = product(enter[...], fp[:size]) + fp[size:]
    y_in = product(leave[...], fq[...]) + product(enter[...], fs[:size]) + fs[size:]
    x_high, x_low = halves(x_in)
    y_high, y_low = halves(y_in)
    left = jnp.concatenate(
        [jnp.concatenate([x_high, y_high], axis=1), jnp.concatenate([x_low, y_low], axis=1)], axis=0
    )
    for i in range(rows):
        both = fold(jnp.dot(left, maps[i], preferred_element_type=jnp.float32), size)
        out[i] = tails[i, size : size + sides] + both[:sides] + both[sides:]


def on_device(levels, planes, rhs, pivot_inv, lower_gain, upper_gain):
    rows, sides, size = rhs.shape
    depth = len(levels)
    span = 3 * size + 2 * sides
    f32 = jnp.float32
    return pl.pallas_call(
        functools.partial(kernel, levels, planes),
        out_shape=jax.ShapeDtypeStruct(rhs.shape, f32),
        in_specs=[pl.BlockSpec(memory_space=pltpu.HBM)] * 4,
        out_specs=pl.BlockSpec(memory_space=pltpu.VMEM),
        scratch_shapes=[
            pltpu.VMEM((rows, sides, size), f32),
            pltpu.VMEM((rows, size, size), f32),
            pltpu.VMEM((rows, size, size), f32),
            pltpu.VMEM((rows, size, size), f32),
            pltpu.VMEM((rows, size + sides, size), f32),
            pltpu.VMEM((rows, 2 * size + sides, size), f32),
            pltpu.VMEM((rows, 2 * size, 2 * size), jnp.bfloat16),
            pltpu.VMEM((depth + 1, 2, span, size), f32),
            pltpu.VMEM((size + sides, size), f32),
            pltpu.VMEM((size, size), f32),
            pltpu.VMEM((size + sides, size), f32),
            pltpu.VMEM((sides, size), f32),
            pltpu.VMEM((sides, size), f32),
            pltpu.VMEM((size + sides, size), f32),
            pltpu.VMEM((sides, size), f32),
            pltpu.VMEM((sides, size), f32),
            pltpu.VMEM((size + sides, size), f32),
            pltpu.SemaphoreType.DMA((4, rows // PIECE)),
            pltpu.SemaphoreType.DMA((depth, PARTS)),
            pltpu.SemaphoreType.DMA((depth, PARTS)),
            pltpu.SemaphoreType.DMA((depth, PARTS)),
            pltpu.SemaphoreType.DMA((depth, PARTS)),
            pltpu.SemaphoreType.DMA((3,)),
            pltpu.SemaphoreType.DMA((3,)),
        ],
        compiler_params=pltpu.CompilerParams(
            collective_id=0, has_side_effects=True, vmem_limit_bytes=40 * 2**20
        ),
    )(rhs, pivot_inv, lower_gain, upper_gain)


def solution(mesh):
    levels = []
    planes = min(4, mesh.shape["wide"])
    for axis, count in (("narrow", mesh.shape["narrow"]), ("wide", mesh.shape["wide"] // planes)):
        stride = 1
        while stride < count:
            levels.append((axis, stride))
            stride *= 2
    placed = P(("wide", "narrow"), None, None)
    return jax.shard_map(
        functools.partial(on_device, tuple(levels), planes),
        mesh=mesh,
        in_specs=(placed,) * 4,
        out_specs=placed,
        check_vma=False,
    )
```

time: 44.3 us -> 43.1 us (0.973)
  Pallas kernels: 38.8 us -> 37.6 us
    pallas_call x1, Pallas kernels: 38.8 us -> 37.6 us  [on_device(): pl.pallas_call(functools.partial(kernel, levels, planes), out_shape=jax.S...]
where the time goes in v2:
time: 43.1 us; the launch traced here: 42.8 us
  Pallas kernels  37.6 us (87%)
  local copies, waits for them, and re-layouts  5.14 us (12%)
    pallas_call x1, Pallas kernels, on_device(): pl.pallas_call(functools.partial(kernel, levels, planes), out_shape=jax.S...  37.6 us
    unnamed x9, local copies, waits for them, and re-layouts  5.14 us

profile of v2, /device:TPU:0, one launch (start us, length us, event | category | flops | bytes accessed | tf_op | source)
XLA Modules:
  0.0 42.8 jit_solution(1410733232990928930)
XLA Ops:
  0.0 0.0 copy-start
  0.0 1.1 %copy-done = f32[12,128,128]{2,1,0:T(8,128)S(1)} copy-done((f32[12,128,128]{2,1,0:T(8,128)S(1)}, f32[12,128,128]{2,1,0:T(8,128)}, u32[]{:S(2)}) %copy-start) | copy-done | bytes 786456
  1.1 0.0 copy-start.1
  1.1 1.1 %copy-done.1 = f32[12,128,128]{2,1,0:T(8,128)S(1)} copy-done((f32[12,128,128]{2,1,0:T(8,128)S(1)}, f32[12,128,128]{2,1,0:T(8,128)}, u32[]{:S(2)}) %copy-start.1) | copy-done | bytes 786456
  2.3 0.0 copy-start.2
  2.3 1.1 %copy-done.2 = f32[12,128,128]{2,1,0:T(8,128)S(1)} copy-done((f32[12,128,128]{2,1,0:T(8,128)S(1)}, f32[12,128,128]{2,1,0:T(8,128)}, u32[]{:S(2)}) %copy-start.2) | copy-done | bytes 786456
  3.4 0.0 copy-start.3
  3.4 1.0 %copy-done.3 = f32[12,64,128]{2,1,0:T(8,128)S(1)} copy-done((f32[12,64,128]{2,1,0:T(8,128)S(1)}, f32[12,64,128]{2,1,0:T(8,128)}, u32[]{:S(2)}) %copy-start.3) | copy-done | bytes 393240
  4.4 37.6 %shard_map.46 = f32[12,64,128]{2,1,0:T(8,128)S(1)} custom-call(f32[12,64,128]{2,1,0:T(8,128)S(1)} %copy-done.3, f32[12,128,128]{2,1,0:T(8,128)S(1)} %copy-done, f32[12,128,128]{2,1,0:T(8,128)S(1)} %copy-done.1, f32[12,128,128]{2,1,0:T(8,128)S(1)} %copy-done.2), custom_call_target="tpu_custom_call" | custom-call | tf_op jit(solution)/shard_map/pallas_call | solution.py:340
  42.0 0.7 %copy.6 = f32[12,64,128]{2,1,0:T(8,128)} copy(f32[12,64,128]{2,1,0:T(8,128)S(1)} %shard_map.46) | data formatting | bytes 786432
Async XLA Ops:
  0.0 1.1 %copy-start = (f32[12,128,128]{2,1,0:T(8,128)S(1)}, f32[12,128,128]{2,1,0:T(8,128)}, u32[]{:S(2)}) copy-start(f32[12,128,128]{2,1,0:T(8,128)} %pivot_hbm.1) | copy-start | bytes 2359300
  1.1 1.1 %copy-start.1 = (f32[12,128,128]{2,1,0:T(8,128)S(1)}, f32[12,128,128]{2,1,0:T(8,128)}, u32[]{:S(2)}) copy-start(f32[12,128,128]{2,1,0:T(8,128)} %lower_hbm.1) | copy-start | bytes 2359300
  2.3 1.1 %copy-start.2 = (f32[12,128,128]{2,1,0:T(8,128)S(1)}, f32[12,128,128]{2,1,0:T(8,128)}, u32[]{:S(2)}) copy-start(f32[12,128,128]{2,1,0:T(8,128)} %upper_hbm.1) | copy-start | bytes 2359300
  3.4 1.0 %copy-start.3 = (f32[12,64,128]{2,1,0:T(8,128)S(1)}, f32[12,64,128]{2,1,0:T(8,128)}, u32[]{:S(2)}) copy-start(f32[12,64,128]{2,1,0:T(8,128)} %rhs_hbm.1) | copy-start | bytes 1179652

commit v3 on v2

--- a/solution.py
+++ b/solution.py
@@ -8,7 +8,7 @@
 from jax.sharding import PartitionSpec as P
 
 MESH = pl.DeviceIdType.MESH
-PIECE = 3
+SEGMENT = 3
 PARTS = 2
 
 
@@ -53,6 +53,9 @@
     ahead,
     tails,
     maps,
+    seg_into,
+    seg_leaves,
+    seg_cross,
     group,
     fp,
     fq,
@@ -77,17 +80,16 @@
     place = {name: lax.axis_index(name) for name in names}
     depth = len(levels)
 
-    loads = {}
-    pieces = rows // PIECE
-    for step in range(pieces):
-        for kind, (source, target) in enumerate(
-            ((rhs_hbm, rhs), (pivot_hbm, pivot), (lower_hbm, lower), (upper_hbm, upper))
-        ):
-            piece = pieces - 1 - step if kind == 3 else step
-            span = pl.ds(piece * PIECE, PIECE)
+    segments = rows // SEGMENT
+    loads = []
+    for kind, (source, target) in enumerate(
+        ((rhs_hbm, rhs), (pivot_hbm, pivot), (lower_hbm, lower), (upper_hbm, upper))
+    ):
+        for piece in range(segments):
+            span = pl.ds(piece * SEGMENT, SEGMENT)
             load = pltpu.make_async_copy(source.at[span], target.at[span], load_sem.at[kind, piece])
             load.start()
-            loads[kind, step] = load
+            loads.append(load)
 
     def partner(level):
         axis, stride = levels[level]
@@ -114,25 +116,59 @@
     def _():
         pl.semaphore_signal(barrier, inc=1, device_id=after, device_id_type=MESH)
 
+    for load in loads[: 2 * segments]:
+        load.wait()
     for i in range(rows):
-        if i % PIECE == 0:
-            for kind in range(4):
-                loads[kind, i // PIECE].wait()
-        scaled = product(rhs[i], pivot[i])
-        if i == 0:
-            front = jnp.concatenate([-lower[0], scaled], axis=0)
-            back = -upper[rows - 1]
-        else:
-            step = product(front, lower[i])
-            front = jnp.concatenate([-step[:size], scaled - step[size:]], axis=0)
-            back = -product(back, upper[rows - 1 - i])
-        ahead[i] = front
-        tails[rows - 1 - i, size + sides :] = back
-    total = front
-    tails[rows - 1, : size + sides] = total
-    for i in range(rows - 2, -1, -1):
-        total = ahead[i] - product(total, upper[i])
-        tails[i, : size + sides] = total
+        ahead[i, size:] = product(rhs[i], pivot[i])
+    for load in loads[2 * segments :]:
+        load.wait()
+
+    starts = [segment * SEGMENT for segment in range(segments)]
+    fronts, backs = [], []
+    for begin in starts:
+        fronts.append(jnp.concatenate([-lower[begin], ahead[begin, size:]], axis=0))
+        ahead[begin, :size] = fronts[-1][:size]
+        backs.append(-upper[begin + SEGMENT - 1])
+        tails[begin + SEGMENT - 1, size + sides :] = backs[-1]
+    for k in range(1, SEGMENT):
+        for s, begin in enumerate(starts):
+            i, j = begin + k, begin + SEGMENT - 1 - k
+            step = product(fronts[s], lower[i])
+            fronts[s] = jnp.concatenate([-step[:size], ahead[i, size:] - step[size:]], axis=0)
+            ahead[i] = fronts[s]
+            backs[s] = -product(backs[s], upper[j])
+            tails[j, size + sides :] = backs[s]
+    totals = list(fronts)
+    for s, begin in enumerate(starts):
+        tails[begin + SEGMENT - 1, : size + sides] = totals[s]
+    for k in range(1, SEGMENT):
+        for s, begin in enumerate(starts):
+            j = begin + SEGMENT - 1 - k
+            totals[s] = ahead[j] - product(totals[s], upper[j])
+            tails[j, : size + sides] = totals[s]
+
+    def compose(front, first_total, first_back, second_front, second_total, second_back):
+        joined = jnp.dot(
+            left_side(front),
+            jnp.concatenate([right_side(second_front[:size]), right_side(second_total[:size])], axis=1),
+            preferred_element_type=jnp.float32,
+        )
+        onward = add_offset(fold(joined[:, : 2 * size], size), second_front[size:])
+        turned = add_offset(fold(joined[:, 2 * size :], size), second_total[size:])
+        turned = jnp.concatenate([turned, second_back], axis=0)
+        returned = product(turned, first_back)
+        return onward, first_total + returned[: size + sides], returned[size + sides :], turned
+
+    def add_offset(value, offset):
+        return jnp.concatenate([value[:size], value[size:] + offset], axis=0)
+
+    spans = [(fronts[s], totals[s], backs[s]) for s in range(segments)]
+    joins = []
+    while len(spans) > 1:
+        made = [compose(*spans[k], *spans[k + 1]) for k in range(0, len(spans), 2)]
+        joins.append([(spans[2 * k][0], made[k][3]) for k in range(len(made))])
+        spans = [one[:3] for one in made]
+    local_front, local_total, local_back = spans[0]
 
     inner = (plane > 0).astype(jnp.int32) + (plane < planes - 1).astype(jnp.int32)
     pl.semaphore_wait(barrier, depth + inner)
@@ -184,13 +220,39 @@
             relay.wait()
 
     side = partner(0)[0]
-    group[0, side, :c0] = ahead[rows - 1, :size]
-    group[0, side, c0:w0] = ahead[rows - 1, size:]
-    group[0, side, w0:n0] = tails[0, : size + sides]
-    group[0, side, n0:] = tails[0, size + sides :]
+    group[0, side, m0:w0] = local_front
+    group[0, side, w0:n0] = local_total
+    group[0, side, n0:] = local_back
     copies = exchange(0)
     for copy in copies:
         copy.start()
+
+    into, leaves, crosses = [None] * segments, [None] * segments, [None] * segments
+    for level, pairs in enumerate(joins):
+        for s in range(segments):
+            front, turned = pairs[s >> (level + 1)]
+            if (s >> level) & 1 == 0:
+                if leaves[s] is None:
+                    more = turned
+                else:
+                    more = product(turned, leaves[s])
+                leaves[s] = more[size + sides :]
+                cross = more[: size + sides]
+                crosses[s] = cross if crosses[s] is None else crosses[s] + cross
+            else:
+                into[s] = front if into[s] is None else add_offset(product(front, into[s][:size]), into[s][size:])
+                if crosses[s] is not None:
+                    crosses[s] = add_offset(product(front, crosses[s][:size]), crosses[s][size:])
+    has_into = [value is not None for value in into]
+    has_leaves = [value is not None for value in leaves]
+    has_cross = [value is not None for value in crosses]
+    for s in range(segments):
+        if has_into[s]:
+            seg_into[s] = into[s]
+        if has_leaves[s]:
+            seg_leaves[s] = leaves[s]
+        if has_cross[s]:
+            seg_cross[s] = crosses[s]
 
     eye = (
         lax.broadcasted_iota(jnp.int32, (size, size), 0) == lax.broadcasted_iota(jnp.int32, (size, size), 1)
@@ -219,20 +281,13 @@
         side = partner(level)[0]
         first, second = group.at[level, 0], group.at[level, 1]
         front = first[m0:w0]
-        joined = jnp.dot(
-            left_side(front),
-            jnp.concatenate([right_side(second[m0:c0]), right_side(second[w0:b0])], axis=1),
-            preferred_element_type=jnp.float32,
+        onward, total, back, turned = compose(
+            front, first[w0:n0], first[n0:], second[m0:w0], second[w0:n0], second[n0:]
         )
-        onward = fold(joined[:, : 2 * size], size)
-        turned = fold(joined[:, 2 * size :], size)
-        turned = jnp.concatenate([turned[:size], turned[size:] + second[b0:n0]], axis=0)
-        returned = product(jnp.concatenate([turned, second[n0:]], axis=0), first[n0:])
         following = partner(level + 1)[0] if level < depth - 1 else 0
-        group[level + 1, following, m0:c0] = onward[:size]
-        group[level + 1, following, c0:w0] = onward[size:] + second[c0:w0]
-        group[level + 1, following, w0:n0] = first[w0:n0] + returned[: size + sides]
-        group[level + 1, following, n0:] = returned[size + sides :]
+        group[level + 1, following, m0:w0] = onward
+        group[level + 1, following, w0:n0] = total
+        group[level + 1, following, n0:] = back
         if level < depth - 1:
             copies = exchange(level + 1)
             for copy in copies:
@@ -260,7 +315,7 @@
 
         @pl.when(side == 0)
         def _():
-            more = product(jnp.concatenate([turned, second[n0:]], axis=0), fq[...])
+            more = product(turned, fq[...])
             fs[...] = fs[...] + more[: size + sides]
             fq[...] = more[size + sides :]
 
@@ -322,14 +377,22 @@
 
     x_in = product(enter[...], fp[:size]) + fp[size:]
     y_in = product(leave[...], fq[...]) + product(enter[...], fs[:size]) + fs[size:]
-    x_high, x_low = halves(x_in)
-    y_high, y_low = halves(y_in)
-    left = jnp.concatenate(
-        [jnp.concatenate([x_high, y_high], axis=1), jnp.concatenate([x_low, y_low], axis=1)], axis=0
-    )
-    for i in range(rows):
-        both = fold(jnp.dot(left, maps[i], preferred_element_type=jnp.float32), size)
-        out[i] = tails[i, size : size + sides] + both[:sides] + both[sides:]
+    for s, begin in enumerate(starts):
+        x_here, y_here = x_in, y_in
+        if has_into[s]:
+            x_here = product(x_in, seg_into[s, :size]) + seg_into[s, size:]
+        if has_leaves[s]:
+            y_here = product(y_in, seg_leaves[s])
+        if has_cross[s]:
+            y_here = y_here + product(x_in, seg_cross[s, :size]) + seg_cross[s, size:]
+        x_high, x_low = halves(x_here)
+        y_high, y_low = halves(y_here)
+        left = jnp.concatenate(
+            [jnp.concatenate([x_high, y_high], axis=1), jnp.concatenate([x_low, y_low], axis=1)], axis=0
+        )
+        for i in range(begin, begin + SEGMENT):
+            both = fold(jnp.dot(left, maps[i], preferred_element_type=jnp.float32), size)
+            out[i] = tails[i, size : size + sides] + both[:sides] + both[sides:]
 
 
 def on_device(levels, planes, rhs, pivot_inv, lower_gain, upper_gain):
@@ -350,6 +413,9 @@
             pltpu.VMEM((rows, size + sides, size), f32),
             pltpu.VMEM((rows, 2 * size + sides, size), f32),
             pltpu.VMEM((rows, 2 * size, 2 * size), jnp.bfloat16),
+            pltpu.VMEM((rows // SEGMENT, size + sides, size), f32),
+            pltpu.VMEM((rows // SEGMENT, size, size), f32),
+            pltpu.VMEM((rows // SEGMENT, size + sides, size), f32),
             pltpu.VMEM((depth + 1, 2, span, size), f32),
             pltpu.VMEM((size + sides, size), f32),
             pltpu.VMEM((size, size), f32),
@@ -360,7 +426,7 @@
             pltpu.VMEM((sides, size), f32),
             pltpu.VMEM((sides, size), f32),
             pltpu.VMEM((size + sides, size), f32),
-            pltpu.SemaphoreType.DMA((4, rows // PIECE)),
+            pltpu.SemaphoreType.DMA((4, rows // SEGMENT)),
             pltpu.SemaphoreType.DMA((depth, PARTS)),
             pltpu.SemaphoreType.DMA((depth, PARTS)),
             pltpu.SemaphoreType.DMA((depth, PARTS)),
@@ -369,7 +435,7 @@
             pltpu.SemaphoreType.DMA((3,)),
         ],
         compiler_params=pltpu.CompilerParams(
-            collective_id=0, has_side_effects=True, vmem_limit_bytes=40 * 2**20
+            collective_id=0, has_side_effects=True, vmem_limit_bytes=63 * 2**20
         ),
     )(rhs, pivot_inv, lower_gain, upper_gain)
 

time: 43.1 us -> 37.4 us (0.87)
  local copies, waits for them, and re-layouts: 5.14 us -> 1.77 us
  Pallas kernels: 37.6 us -> 35.5 us
    unnamed x9 -> x1, local copies, waits for them, and re-layouts: 5.14 us -> 1.77 us
    pallas_call x1, Pallas kernels: 37.6 us -> 35.5 us  [on_device(): pl.pallas_call(functools.partial(kernel, levels, planes), out_shape=jax.S...]
where the time goes in v3:
time: 37.4 us; the launch traced here: 37.2 us
  Pallas kernels  35.5 us (95%)
  local copies, waits for them, and re-layouts  1.77 us (5%)
    pallas_call x1, Pallas kernels, on_device(): pl.pallas_call(functools.partial(kernel, levels, planes), out_shape=jax.S...  35.5 us
    unnamed x1, local copies, waits for them, and re-layouts  1.77 us

profile of v3, /device:TPU:0, one launch (start us, length us, event | category | flops | bytes accessed | tf_op | source)
XLA Modules:
  0.0 37.2 jit_solution(15418777114424344233)
XLA Ops:
  0.0 35.5 %shard_map.46 = f32[12,64,128]{2,1,0:T(8,128)} custom-call(f32[12,64,128]{2,1,0:T(8,128)} %rhs_hbm.1, f32[12,128,128]{2,1,0:T(8,128)} %pivot_hbm.1, f32[12,128,128]{2,1,0:T(8,128)} %lower_hbm.1, f32[12,128,128]{2,1,0:T(8,128)} %upper_hbm.1), custom_call_target="tpu_custom_call" | custom-call | tf_op jit(solution)/shard_map/pallas_call | solution.py:403
  35.5 1.8 %copy.6 = f32[12,64,128]{2,1,0:T(8,128)} copy(f32[12,64,128]{2,1,0:T(8,128)} %shard_map.46) | data formatting | bytes 786432

commit v4 on v3

--- a/solution.py
+++ b/solution.py
@@ -339,7 +339,7 @@
             reach = product(enter[...], mine[m0:c0]) + mine[c0:w0]
             enter_on[...] = reach
             enter_right.start()
-        if index == planes // 2 - 1:
+        if index == planes - 2:
             if index > 0:
                 partial = product(enter[...], mine[w0:b0]) + mine[b0:n0]
             met_left.wait_recv()
@@ -373,7 +373,7 @@
         met_left.wait_send()
 
     for index in range(planes):
-        pl.when(plane == index)(functools.partial(step_left if index < planes // 2 else step_right, index))
+        pl.when(plane == index)(functools.partial(step_left if index < planes - 1 else step_right, index))
 
     x_in = product(enter[...], fp[:size]) + fp[size:]
     y_in = product(leave[...], fq[...]) + product(enter[...], fs[:size]) + fs[size:]
@@ -402,7 +402,7 @@
     f32 = jnp.float32
     return pl.pallas_call(
         functools.partial(kernel, levels, planes),
-        out_shape=jax.ShapeDtypeStruct(rhs.shape, f32),
+        out_shape=pltpu.VMEM(rhs.shape, f32),
         in_specs=[pl.BlockSpec(memory_space=pltpu.HBM)] * 4,
         out_specs=pl.BlockSpec(memory_space=pltpu.VMEM),
         scratch_shapes=[
@@ -435,7 +435,7 @@
             pltpu.SemaphoreType.DMA((3,)),
         ],
         compiler_params=pltpu.CompilerParams(
-            collective_id=0, has_side_effects=True, vmem_limit_bytes=63 * 2**20
+            collective_id=0, has_side_effects=True, vmem_limit_bytes=62 * 2**20
         ),
     )(rhs, pivot_inv, lower_gain, upper_gain)
 

time: 37.4 us -> 34.9 us (0.933)
  Pallas kernels: 35.5 us -> 34 us
  local copies, waits for them, and re-layouts: 1.77 us -> 0.75 us
    pallas_call x1, Pallas kernels: 35.5 us -> 34 us  [on_device(): pl.pallas_call(functools.partial(kernel, levels, planes), out_shape=pltpu...]
    unnamed x1, local copies, waits for them, and re-layouts: 1.77 us -> 0.75 us
where the time goes in v4:
time: 34.9 us; the launch traced here: 34.8 us
  Pallas kernels  34 us (97%)
  local copies, waits for them, and re-layouts  0.75 us (2%)
    pallas_call x1, Pallas kernels, on_device(): pl.pallas_call(functools.partial(kernel, levels, planes), out_shape=pltpu...  34 us
    unnamed x1, local copies, waits for them, and re-layouts  0.75 us

profile of v4, /device:TPU:0, one launch (start us, length us, event | category | flops | bytes accessed | tf_op | source)
XLA Modules:
  0.0 34.8 jit_solution(18440472618946259767)
XLA Ops:
  0.0 34.0 %shard_map.46 = f32[12,64,128]{2,1,0:T(8,128)S(1)} custom-call(f32[12,64,128]{2,1,0:T(8,128)} %rhs_hbm.1, f32[12,128,128]{2,1,0:T(8,128)} %pivot_hbm.1, f32[12,128,128]{2,1,0:T(8,128)} %lower_hbm.1, f32[12,128,128]{2,1,0:T(8,128)} %upper_hbm.1), custom_call_target="tpu_custom_call" | custom-call | tf_op jit(solution)/shard_map/pallas_call | solution.py:403
  34.0 0.7 %copy.6 = f32[12,64,128]{2,1,0:T(8,128)} copy(f32[12,64,128]{2,1,0:T(8,128)S(1)} %shard_map.46) | data formatting | bytes 786432

commit v5 on v4

--- a/solution.py
+++ b/solution.py
@@ -56,6 +56,8 @@
     seg_into,
     seg_leaves,
     seg_cross,
+    y_parts,
+    y_maps,
     group,
     fp,
     fq,
@@ -306,12 +308,8 @@
 
         if level == 0:
             for i in range(rows):
-                w_high, w_low = halves(tails[i, :size])
-                n_high, n_low = halves(tails[i, size + sides :])
-                maps[i] = jnp.concatenate(
-                    [jnp.concatenate([w_high, w_low], axis=1), jnp.concatenate([n_high, n_low], axis=1)],
-                    axis=0,
-                )
+                maps[0, i] = right_side(tails[i, :size])
+                maps[1, i] = right_side(tails[i, size + sides :])
 
         @pl.when(side == 0)
         def _():
@@ -327,6 +325,27 @@
             more = product(front, fs[:size])
             fs[size:] = fs[size:] + more[size:]
             fs[:size] = more[:size]
+
+    def prepare():
+        x_in = product(enter[...], fp[:size]) + fp[size:]
+        y_part = product(enter[...], fs[:size]) + fs[size:]
+        for s, begin in enumerate(starts):
+            x_here = x_in
+            if has_into[s]:
+                x_here = product(x_in, seg_into[s, :size]) + seg_into[s, size:]
+            y_here = y_part
+            back = fq[...]
+            if has_leaves[s]:
+                both = product(jnp.concatenate([y_part, back], axis=0), seg_leaves[s])
+                y_here, back = both[:sides], both[sides:]
+            if has_cross[s]:
+                y_here = y_here + product(x_in, seg_cross[s, :size]) + seg_cross[s, size:]
+            y_parts[s] = y_here
+            y_maps[s] = right_side(back)
+            left = left_side(x_here)
+            for i in range(begin, begin + SEGMENT):
+                more = jnp.dot(left, maps[0, i], preferred_element_type=jnp.float32)
+                tails[i, size : size + sides] = tails[i, size : size + sides] + fold(more, size)
 
     mine = group.at[depth, 0]
 
@@ -347,10 +366,14 @@
         else:
             if index > 0:
                 partial = product(enter[...], mine[w0:b0]) + mine[b0:n0]
+            prepare()
             leave_left.wait_recv()
         if index > 0:
             leave_on[...] = product(leave[...], mine[n0:]) + partial
             leave_left.start()
+        if index == planes - 2:
+            prepare()
+        if index > 0:
             leave_left.wait_send()
         enter_right.wait_send()
 
@@ -370,29 +393,19 @@
             enter_right.wait_send()
         else:
             leave[...] = jnp.zeros((sides, size), jnp.float32)
+        prepare()
         met_left.wait_send()
 
     for index in range(planes):
         pl.when(plane == index)(functools.partial(step_left if index < planes - 1 else step_right, index))
 
-    x_in = product(enter[...], fp[:size]) + fp[size:]
-    y_in = product(leave[...], fq[...]) + product(enter[...], fs[:size]) + fs[size:]
+    left = left_side(leave[...])
     for s, begin in enumerate(starts):
-        x_here, y_here = x_in, y_in
-        if has_into[s]:
-            x_here = product(x_in, seg_into[s, :size]) + seg_into[s, size:]
-        if has_leaves[s]:
-            y_here = product(y_in, seg_leaves[s])
-        if has_cross[s]:
-            y_here = y_here + product(x_in, seg_cross[s, :size]) + seg_cross[s, size:]
-        x_high, x_low = halves(x_here)
-        y_high, y_low = halves(y_here)
-        left = jnp.concatenate(
-            [jnp.concatenate([x_high, y_high], axis=1), jnp.concatenate([x_low, y_low], axis=1)], axis=0
-        )
+        y_here = fold(jnp.dot(left, y_maps[s], preferred_element_type=jnp.float32), size) + y_parts[s]
+        there = left_side(y_here)
         for i in range(begin, begin + SEGMENT):
-            both = fold(jnp.dot(left, maps[i], preferred_element_type=jnp.float32), size)
-            out[i] = tails[i, size : size + sides] + both[:sides] + both[sides:]
+            more = jnp.dot(there, maps[1, i], preferred_element_type=jnp.float32)
+            out[i] = tails[i, size : size + sides] + fold(more, size)
 
 
 def on_device(levels, planes, rhs, pivot_inv, lower_gain, upper_gain):
@@ -412,10 +425,12 @@
             pltpu.VMEM((rows, size, size), f32),
             pltpu.VMEM((rows, size + sides, size), f32),
             pltpu.VMEM((rows, 2 * size + sides, size), f32),
-            pltpu.VMEM((rows, 2 * size, 2 * size), jnp.bfloat16),
+            pltpu.VMEM((2, rows, 2 * size, 2 * size), jnp.bfloat16),
             pltpu.VMEM((rows // SEGMENT, size + sides, size), f32),
             pltpu.VMEM((rows // SEGMENT, size, size), f32),
             pltpu.VMEM((rows // SEGMENT, size + sides, size), f32),
+            pltpu.VMEM((rows // SEGMENT, sides, size), f32),
+            pltpu.VMEM((rows // SEGMENT, 2 * size, 2 * size), jnp.bfloat16),
             pltpu.VMEM((depth + 1, 2, span, size), f32),
             pltpu.VMEM((size + sides, size), f32),
             pltpu.VMEM((size, size), f32),

time: 34.9 us -> 34.7 us (level)
  no operation moved by 1% of the time
where the time goes in v5:
time: 34.7 us; the launch traced here: 34.5 us
  Pallas kernels  33.8 us (97%)
  local copies, waits for them, and re-layouts  0.75 us (2%)
    pallas_call x1, Pallas kernels, on_device(): pl.pallas_call(functools.partial(kernel, levels, planes), out_shape=pltpu...  33.8 us
    unnamed x1, local copies, waits for them, and re-layouts  0.75 us

profile of v5, /device:TPU:0, one launch (start us, length us, event | category | flops | bytes accessed | tf_op | source)
XLA Modules:
  0.0 34.5 jit_solution(4932785780279751370)
XLA Ops:
  0.0 33.8 %shard_map.46 = f32[12,64,128]{2,1,0:T(8,128)S(1)} custom-call(f32[12,64,128]{2,1,0:T(8,128)} %rhs_hbm.1, f32[12,128,128]{2,1,0:T(8,128)} %pivot_hbm.1, f32[12,128,128]{2,1,0:T(8,128)} %lower_hbm.1, f32[12,128,128]{2,1,0:T(8,128)} %upper_hbm.1), custom_call_target="tpu_custom_call" | custom-call | tf_op jit(solution)/shard_map/pallas_call | solution.py:416
  33.8 0.7 %copy.6 = f32[12,64,128]{2,1,0:T(8,128)} copy(f32[12,64,128]{2,1,0:T(8,128)S(1)} %shard_map.46) | data formatting | bytes 786432

commit v6 on v5

--- a/solution.py
+++ b/solution.py
@@ -9,7 +9,6 @@
 
 MESH = pl.DeviceIdType.MESH
 SEGMENT = 3
-PARTS = 2
 
 
 def halves(value):
@@ -71,8 +70,6 @@
     load_sem,
     send_sem,
     recv_sem,
-    pass_send_sem,
-    pass_recv_sem,
     chain_send_sem,
     chain_recv_sem,
 ):
@@ -104,7 +101,6 @@
     plane = lax.div(place["wide"], hop)
     before = (place["wide"] - hop, place["narrow"])
     after = (place["wide"] + hop, place["narrow"])
-    sibling = (place["wide"], 1 - place["narrow"])
 
     barrier = pltpu.get_barrier_semaphore()
     for level in range(depth):
@@ -149,7 +145,7 @@
             totals[s] = ahead[j] - product(totals[s], upper[j])
             tails[j, : size + sides] = totals[s]
 
-    def compose(front, first_total, first_back, second_front, second_total, second_back):
+    def compose(front, first_total, second_front, second_total, get_backs):
         joined = jnp.dot(
             left_side(front),
             jnp.concatenate([right_side(second_front[:size]), right_side(second_total[:size])], axis=1),
@@ -157,6 +153,7 @@
         )
         onward = add_offset(fold(joined[:, : 2 * size], size), second_front[size:])
         turned = add_offset(fold(joined[:, 2 * size :], size), second_total[size:])
+        first_back, second_back = get_backs()
         turned = jnp.concatenate([turned, second_back], axis=0)
         returned = product(turned, first_back)
         return onward, first_total + returned[: size + sides], returned[size + sides :], turned
@@ -167,7 +164,10 @@
     spans = [(fronts[s], totals[s], backs[s]) for s in range(segments)]
     joins = []
     while len(spans) > 1:
-        made = [compose(*spans[k], *spans[k + 1]) for k in range(0, len(spans), 2)]
+        made = [
+            compose(*spans[k][:2], *spans[k + 1][:2], lambda k=k: (spans[k][2], spans[k + 1][2]))
+            for k in range(0, len(spans), 2)
+        ]
         joins.append([(spans[2 * k][0], made[k][3]) for k in range(len(made))])
         spans = [one[:3] for one in made]
     local_front, local_total, local_back = spans[0]
@@ -175,15 +175,8 @@
     inner = (plane > 0).astype(jnp.int32) + (plane < planes - 1).astype(jnp.int32)
     pl.semaphore_wait(barrier, depth + inner)
 
-    part = end // (2 * PARTS)
-
     def exchange(level):
         side, other = partner(level)
-        if levels[level][0] == "narrow":
-            spans = [pl.ds(0, end)]
-        else:
-            begin = place["narrow"] * (end // 2)
-            spans = [pl.ds(pl.multiple_of(begin + k * part, part), part) for k in range(PARTS)]
         return [
             pltpu.make_async_remote_copy(
                 src_ref=group.at[level, side, span],
@@ -193,33 +186,8 @@
                 device_id=other,
                 device_id_type=MESH,
             )
-            for k, span in enumerate(spans)
+            for k, span in enumerate((pl.ds(m0, n0 - m0), pl.ds(n0, end - n0)))
         ]
-
-    def finish(level, copies):
-        if levels[level][0] == "narrow":
-            copies[0].wait()
-            return
-        side = partner(level)[0]
-        begin = place["narrow"] * (end // 2)
-        relays = []
-        for k, copy in enumerate(copies):
-            copy.wait_recv()
-            span = pl.ds(pl.multiple_of(begin + k * part, part), part)
-            relay = pltpu.make_async_remote_copy(
-                src_ref=group.at[level, 1 - side, span],
-                dst_ref=group.at[level, 1 - side, span],
-                send_sem=pass_send_sem.at[level, k],
-                recv_sem=pass_recv_sem.at[level, k],
-                device_id=sibling,
-                device_id_type=MESH,
-            )
-            relay.start()
-            relays.append(relay)
-        for copy in copies:
-            copy.wait_send()
-        for relay in relays:
-            relay.wait()
 
     side = partner(0)[0]
     group[0, side, m0:w0] = local_front
@@ -278,14 +246,23 @@
     met_left = hand(1, met_on, met, before)
     leave_left = hand(2, leave_on, leave, before)
 
+    def backs_of(copies, first, second):
+        def get_backs():
+            copies[1].wait_recv()
+            return first[n0:], second[n0:]
+
+        return get_backs
+
     for level in range(depth):
-        finish(level, copies)
+        copies[0].wait_recv()
         side = partner(level)[0]
         first, second = group.at[level, 0], group.at[level, 1]
         front = first[m0:w0]
         onward, total, back, turned = compose(
-            front, first[w0:n0], first[n0:], second[m0:w0], second[w0:n0], second[n0:]
+            front, first[w0:n0], second[m0:w0], second[w0:n0], backs_of(copies, first, second)
         )
+        for copy in copies:
+            copy.wait_send()
         following = partner(level + 1)[0] if level < depth - 1 else 0
         group[level + 1, following, m0:w0] = onward
         group[level + 1, following, w0:n0] = total
@@ -442,10 +419,8 @@
             pltpu.VMEM((sides, size), f32),
             pltpu.VMEM((size + sides, size), f32),
             pltpu.SemaphoreType.DMA((4, rows // SEGMENT)),
-            pltpu.SemaphoreType.DMA((depth, PARTS)),
-            pltpu.SemaphoreType.DMA((depth, PARTS)),
-            pltpu.SemaphoreType.DMA((depth, PARTS)),
-            pltpu.SemaphoreType.DMA((depth, PARTS)),
+            pltpu.SemaphoreType.DMA((depth, 2)),
+            pltpu.SemaphoreType.DMA((depth, 2)),
             pltpu.SemaphoreType.DMA((3,)),
             pltpu.SemaphoreType.DMA((3,)),
         ],

time: 34.7 us -> 37.8 us (1.089)
  Pallas kernels: 33.8 us -> 36.9 us
    pallas_call x1, Pallas kernels: 33.8 us -> 36.9 us  [on_device(): pl.pallas_call(functools.partial(kernel, levels, planes), out_shape=pltpu...]
where the time goes in v6:
time: 37.8 us; the launch traced here: 37.7 us
  Pallas kernels  36.9 us (98%)
  local copies, waits for them, and re-layouts  0.75 us (2%)
    pallas_call x1, Pallas kernels, on_device(): pl.pallas_call(functools.partial(kernel, levels, planes), out_shape=pltpu...  36.9 us

profile of v6, /device:TPU:0, one launch (start us, length us, event | category | flops | bytes accessed | tf_op | source)
XLA Modules:
  0.0 37.7 jit_solution(5516021985727213095)
XLA Ops:
  0.0 36.9 %shard_map.46 = f32[12,64,128]{2,1,0:T(8,128)S(1)} custom-call(f32[12,64,128]{2,1,0:T(8,128)} %rhs_hbm.1, f32[12,128,128]{2,1,0:T(8,128)} %pivot_hbm.1, f32[12,128,128]{2,1,0:T(8,128)} %lower_hbm.1, f32[12,128,128]{2,1,0:T(8,128)} %upper_hbm.1), custom_call_target="tpu_custom_call" | custom-call | tf_op jit(solution)/shard_map/pallas_call | solution.py:393
  37.0 0.7 %copy.6 = f32[12,64,128]{2,1,0:T(8,128)} copy(f32[12,64,128]{2,1,0:T(8,128)S(1)} %shard_map.46) | data formatting | bytes 786432

commit v7 on v5

--- a/solution.py
+++ b/solution.py
@@ -9,7 +9,7 @@
 
 MESH = pl.DeviceIdType.MESH
 SEGMENT = 3
-PARTS = 2
+PARTS = 4
 
 
 def halves(value):
@@ -149,7 +149,7 @@
             totals[s] = ahead[j] - product(totals[s], upper[j])
             tails[j, : size + sides] = totals[s]
 
-    def compose(front, first_total, first_back, second_front, second_total, second_back):
+    def compose(front, first_total, second_front, second_total, get_backs):
         joined = jnp.dot(
             left_side(front),
             jnp.concatenate([right_side(second_front[:size]), right_side(second_total[:size])], axis=1),
@@ -157,6 +157,7 @@
         )
         onward = add_offset(fold(joined[:, : 2 * size], size), second_front[size:])
         turned = add_offset(fold(joined[:, 2 * size :], size), second_total[size:])
+        first_back, second_back = get_backs()
         turned = jnp.concatenate([turned, second_back], axis=0)
         returned = product(turned, first_back)
         return onward, first_total + returned[: size + sides], returned[size + sides :], turned
@@ -167,7 +168,10 @@
     spans = [(fronts[s], totals[s], backs[s]) for s in range(segments)]
     joins = []
     while len(spans) > 1:
-        made = [compose(*spans[k], *spans[k + 1]) for k in range(0, len(spans), 2)]
+        made = [
+            compose(*spans[k][:2], *spans[k + 1][:2], lambda k=k: (spans[k][2], spans[k + 1][2]))
+            for k in range(0, len(spans), 2)
+        ]
         joins.append([(spans[2 * k][0], made[k][3]) for k in range(len(made))])
         spans = [one[:3] for one in made]
     local_front, local_total, local_back = spans[0]
@@ -176,14 +180,16 @@
     pl.semaphore_wait(barrier, depth + inner)
 
     part = end // (2 * PARTS)
+
+    def wave(k):
+        return pl.ds(pl.multiple_of((2 * k + place["narrow"]) * part, part), part)
 
     def exchange(level):
         side, other = partner(level)
         if levels[level][0] == "narrow":
             spans = [pl.ds(0, end)]
         else:
-            begin = place["narrow"] * (end // 2)
-            spans = [pl.ds(pl.multiple_of(begin + k * part, part), part) for k in range(PARTS)]
+            spans = [wave(k) for k in range(PARTS)]
         return [
             pltpu.make_async_remote_copy(
                 src_ref=group.at[level, side, span],
@@ -199,16 +205,14 @@
     def finish(level, copies):
         if levels[level][0] == "narrow":
             copies[0].wait()
-            return
+            return None
         side = partner(level)[0]
-        begin = place["narrow"] * (end // 2)
         relays = []
         for k, copy in enumerate(copies):
             copy.wait_recv()
-            span = pl.ds(pl.multiple_of(begin + k * part, part), part)
             relay = pltpu.make_async_remote_copy(
-                src_ref=group.at[level, 1 - side, span],
-                dst_ref=group.at[level, 1 - side, span],
+                src_ref=group.at[level, 1 - side, wave(k)],
+                dst_ref=group.at[level, 1 - side, wave(k)],
                 send_sem=pass_send_sem.at[level, k],
                 recv_sem=pass_recv_sem.at[level, k],
                 device_id=sibling,
@@ -216,10 +220,9 @@
             )
             relay.start()
             relays.append(relay)
-        for copy in copies:
-            copy.wait_send()
-        for relay in relays:
-            relay.wait()
+        for relay in relays[:-1]:
+            relay.wait_recv()
+        return relays
 
     side = partner(0)[0]
     group[0, side, m0:w0] = local_front
@@ -278,14 +281,25 @@
     met_left = hand(1, met_on, met, before)
     leave_left = hand(2, leave_on, leave, before)
 
+    def backs_of(relays, first, second):
+        def get_backs():
+            if relays is not None:
+                relays[-1].wait_recv()
+            return first[n0:], second[n0:]
+
+        return get_backs
+
     for level in range(depth):
-        finish(level, copies)
+        relays = finish(level, copies)
         side = partner(level)[0]
         first, second = group.at[level, 0], group.at[level, 1]
         front = first[m0:w0]
         onward, total, back, turned = compose(
-            front, first[w0:n0], first[n0:], second[m0:w0], second[w0:n0], second[n0:]
+            front, first[w0:n0], second[m0:w0], second[w0:n0], backs_of(relays, first, second)
         )
+        if relays is not None:
+            for copy in copies + relays:
+                copy.wait_send()
         following = partner(level + 1)[0] if level < depth - 1 else 0
         group[level + 1, following, m0:w0] = onward
         group[level + 1, following, w0:n0] = total

time: 34.7 us -> 34.5 us (level)
  no operation moved by 1% of the time
where the time goes in v7:
time: 34.5 us; the launch traced here: 34.4 us
  Pallas kernels  33.6 us (97%)
  local copies, waits for them, and re-layouts  0.75 us (2%)
    pallas_call x1, Pallas kernels, on_device(): pl.pallas_call(functools.partial(kernel, levels, planes), out_shape=pltpu...  33.6 us
    unnamed x1, local copies, waits for them, and re-layouts  0.75 us

profile of v7, /device:TPU:0, one launch (start us, length us, event | category | flops | bytes accessed | tf_op | source)
XLA Modules:
  0.0 34.4 jit_solution(10749213451265995053)
XLA Ops:
  0.0 33.6 %shard_map.46 = f32[12,64,128]{2,1,0:T(8,128)S(1)} custom-call(f32[12,64,128]{2,1,0:T(8,128)} %rhs_hbm.1, f32[12,128,128]{2,1,0:T(8,128)} %pivot_hbm.1, f32[12,128,128]{2,1,0:T(8,128)} %lower_hbm.1, f32[12,128,128]{2,1,0:T(8,128)} %upper_hbm.1), custom_call_target="tpu_custom_call" | custom-call | tf_op jit(solution)/shard_map/pallas_call | solution.py:430
  33.6 0.7 %copy.6 = f32[12,64,128]{2,1,0:T(8,128)} copy(f32[12,64,128]{2,1,0:T(8,128)S(1)} %shard_map.46) | data formatting | bytes 786432

commit v8 on v5

--- a/solution.py
+++ b/solution.py
@@ -275,7 +275,9 @@
         )
 
     enter_right = hand(0, enter_on, enter, after)
-    met_left = hand(1, met_on, met, before)
+    share = pl.ds(pl.multiple_of(place["narrow"] * ((size + sides) // 2), 8), (size + sides) // 2)
+    met_left = hand(1, met_on.at[share], met.at[share], before)
+    met_across = hand(3, met.at[share], met.at[share], sibling)
     leave_left = hand(2, leave_on, leave, before)
 
     for level in range(depth):
@@ -362,6 +364,8 @@
             if index > 0:
                 partial = product(enter[...], mine[w0:b0]) + mine[b0:n0]
             met_left.wait_recv()
+            met_across.start()
+            met_across.wait()
             leave[...] = product(reach, met[:size]) + met[size:]
         else:
             if index > 0:
@@ -378,21 +382,8 @@
         enter_right.wait_send()
 
     def step_right(index):
-        if index < planes - 1:
-            met_left.wait_recv()
-            turned = product(mine[m0:w0], met[:size])
-            turned = jnp.concatenate([turned[:size], turned[size:] + met[size:]], axis=0)
-            met_on[...] = product(turned, mine[n0:]) + mine[w0:n0]
-            met_left.start()
         enter_right.wait_recv()
-        if index < planes - 1:
-            reach = product(enter[...], mine[m0:c0]) + mine[c0:w0]
-            enter_on[...] = reach
-            enter_right.start()
-            leave[...] = product(reach, met[:size]) + met[size:]
-            enter_right.wait_send()
-        else:
-            leave[...] = jnp.zeros((sides, size), jnp.float32)
+        leave[...] = jnp.zeros((sides, size), jnp.float32)
         prepare()
         met_left.wait_send()
 
@@ -446,8 +437,8 @@
             pltpu.SemaphoreType.DMA((depth, PARTS)),
             pltpu.SemaphoreType.DMA((depth, PARTS)),
             pltpu.SemaphoreType.DMA((depth, PARTS)),
-            pltpu.SemaphoreType.DMA((3,)),
-            pltpu.SemaphoreType.DMA((3,)),
+            pltpu.SemaphoreType.DMA((4,)),
+            pltpu.SemaphoreType.DMA((4,)),
         ],
         compiler_params=pltpu.CompilerParams(
             collective_id=0, has_side_effects=True, vmem_limit_bytes=62 * 2**20

time: 34.7 us -> 35.6 us (1.026)
  Pallas kernels: 33.8 us -> 34.7 us
    pallas_call x1, Pallas kernels: 33.8 us -> 34.7 us  [on_device(): pl.pallas_call(functools.partial(kernel, levels, planes), out_shape=pltpu...]
where the time goes in v8:
time: 35.6 us; the launch traced here: 35.4 us
  Pallas kernels  34.7 us (97%)
  local copies, waits for them, and re-layouts  0.75 us (2%)
    pallas_call x1, Pallas kernels, on_device(): pl.pallas_call(functools.partial(kernel, levels, planes), out_shape=pltpu...  34.7 us
    unnamed x1, local copies, waits for them, and re-layouts  0.75 us

profile of v8, /device:TPU:0, one launch (start us, length us, event | category | flops | bytes accessed | tf_op | source)
XLA Modules:
  0.0 35.4 jit_solution(15461742572173600073)
XLA Ops:
  0.0 34.7 %shard_map.46 = f32[12,64,128]{2,1,0:T(8,128)S(1)} custom-call(f32[12,64,128]{2,1,0:T(8,128)} %rhs_hbm.1, f32[12,128,128]{2,1,0:T(8,128)} %pivot_hbm.1, f32[12,128,128]{2,1,0:T(8,128)} %lower_hbm.1, f32[12,128,128]{2,1,0:T(8,128)} %upper_hbm.1), custom_call_target="tpu_custom_call" | custom-call | tf_op jit(solution)/shard_map/pallas_call | solution.py:407
  34.7 0.7 %copy.6 = f32[12,64,128]{2,1,0:T(8,128)} copy(f32[12,64,128]{2,1,0:T(8,128)S(1)} %shard_map.46) | data formatting | bytes 786432
